TPU v7x, 32 devices: a whole 2x2x4 slice. The times are simulated.
32 devices in a mesh: str: 16 (over z, y, x), chol: 2 (over core).
Axes of the slice: x: 2, y: 2, z: 4, core: 2. Of those that a mesh axis runs over, the one named last changes fastest.
Arguments:
- amplitudes: bfloat16 [4, 2048, 2048], P(None, 'str'), may hold values from -6 to 6
- alpha_values: bfloat16 [2, 16, 8, 128, 128], P('chol'), may hold values from -0.1875 to 0.1875
- alpha_cols: int32 [2, 16, 8], P('chol'), may hold values from 0 to 15, all different within a row
- beta_values: bfloat16 [2, 16, 8, 128, 128], P('chol'), may hold values from -0.1875 to 0.1875
- beta_cols: int32 [2, 16, 8], P('chol'), may hold values from 0 to 15, all different within a row
Outputs:
- sigma: float32 [4, 2048, 2048], P(None, 'chol', 'str')
Inputs may be any that keep to these rules, and one draw needn't show every extreme that they name: `alpha_cols`: within one block row the 8 block columns are distinct. `beta_cols`: within one block row the 8 block columns are distinct.
All inputs are finite; a program needn't handle non-finite values.
Results may differ from a plain program's by a relative error of at most 0.0029.
Values may be sent and summed in bfloat16 or wider, within the bound.
A program may use at most 128 MiB of HBM per device.

v0:
```python
import functools

import jax
import jax.numpy as jnp
from jax import lax
from jax.experimental import pallas as pl
from jax.experimental.pallas import tpu as pltpu
from jax.sharding import PartitionSpec as P

MESH = pl.DeviceIdType.MESH


def partner(me, step, count):
    if count % 2:
        return (me + 1 + step) % count
    half = count // 2
    side, place = me // half, me % half
    here = step // half
    other = (side + 1 + here) % 2
    return other * half + (place + step + here) % half


def kernel(
    n, nchol, nvec, nblk, nnz, blk,
    acols, bcols, amp_hbm, aval_hbm, bval_hbm, out_hbm,
    amp, aval, bval, send, tsend, trecv, out, *rest,
):
    recv = rest[:nvec]
    amp_sem, aval_sem, bval_sem, send_sem, recv_sem, tsend_sem, trecv_sem, out_sem = rest[nvec:]
    me, core = lax.axis_index("str"), lax.axis_index("chol")
    share = nblk // nchol

    barrier = pltpu.get_barrier_semaphore()

    def greet(step, carry):
        pl.semaphore_signal(
            barrier, inc=1, device_id={"str": (me + 1 + step) % n, "chol": core}, device_id_type=MESH
        )
        return carry

    lax.fori_loop(0, n - 1, greet, 0)
    for o in range(1, nchol):
        pl.semaphore_signal(
            barrier, inc=1, device_id={"str": me, "chol": (core + o) % nchol}, device_id_type=MESH
        )
    def load_amp(c):
        return pltpu.make_async_copy(
            amp_hbm.at[:, :, pl.ds(pl.multiple_of(c * blk, blk), blk)], amp.at[c], amp_sem.at[c]
        )

    def start_amp(c, carry):
        load_amp(c).start()
        return carry

    def wait_amp(c, carry):
        load_amp(c).wait()
        return carry

    lax.fori_loop(0, nblk, start_amp, 0)

    def load_beta(step, j):
        return pltpu.make_async_copy(bval_hbm.at[j], bval.at[j], bval_sem.at[step])

    def start_beta(step, carry):
        load_beta(step, partner(me, step, n)).start()
        return carry

    lax.fori_loop(0, n - 1, start_beta, 0)
    load_beta(n - 1, me).start()
    load_alpha = pltpu.make_async_copy(aval_hbm, aval, aval_sem)

    lax.fori_loop(0, nblk, wait_amp, 0)
    def beta_block(step, j):
        load_beta(step, j).wait()
        total = None
        for m in range(0, nnz, 2):
            left, right = [], []
            for b in range(m, min(m + 2, nnz)):
                left.append(amp[bcols[b, j]].reshape(nvec * blk, blk))
                right.append(bval[j, b])
            part = lax.dot_general(
                jnp.concatenate(left, axis=1), jnp.concatenate(right, axis=1),
                (((1,), (1,)), ((), ())), preferred_element_type=jnp.float32,
            )
            total = part if total is None else total + part
        return total.astype(jnp.bfloat16).reshape(nvec, blk, blk)

    def give(r, step):
        return pltpu.make_async_remote_copy(
            src_ref=send.at[r, step],
            dst_ref=recv[r].at[me],
            send_sem=send_sem.at[r],
            recv_sem=recv_sem.at[r],
            device_id={"str": partner(me, step, n), "chol": core},
            device_id_type=MESH,
        )

    def beta_step(step, carry):
        half = beta_block(step, partner(me, step, n))
        for r in range(nvec):
            send[r, step] = half[r]
        return carry

    def beta_send(step, carry):
        beta_step(step, carry)
        give(0, step).start()
        return carry

    def beta_both(step, carry):
        beta_step(step, carry)
        give(0, step).start()
        if nvec > 1:
            give(1, step - far).start()
        if nvec == 2:
            give(1, step).start()
        return carry

    far = n // 2 if n % 2 == 0 else n - 1
    near = n - 1 - far
    lead = min(1, far)
    lax.fori_loop(0, lead, beta_step, 0)
    pl.semaphore_wait(barrier, n - 1 + nchol - 1)
    for step in range(lead):
        give(0, step).start()
    lax.fori_loop(lead, far, beta_send, 0)
    lax.fori_loop(far, n - 1, beta_both, 0)
    for r in range(1, nvec):
        def start_both(step, carry, r=r):
            give(r - 1, far + step).start()
            if r == nvec - 1:
                give(r, far + step).start()
            give(r, step).start()
            return carry

        def start_far(step, carry, r=r):
            give(r, step).start()
            return carry

        if r > 1:
            lax.fori_loop(0, near, start_both, 0)
        lax.fori_loop(near, far, start_far, 0)
    load_alpha.start()

    mine = beta_block(n - 1, me)
    for r in range(nvec):
        recv[r][me] = mine[r]
    load_alpha.wait()

    def alpha_block(r, i):
        left = jnp.concatenate([aval[i, m] for m in range(nnz)], axis=1)
        right = jnp.concatenate([recv[r][acols[m, i]] for m in range(nnz)], axis=0)
        return jnp.dot(left, right, preferred_element_type=jnp.float32)

    def alpha_rows(to, r, first):
        group = max(g for g in (4, 2, 1) if share % g == 0)

        def some(at, carry):
            for b in range(group):
                row = at * group + b
                to[pl.ds(pl.multiple_of(row * blk, blk), blk), :] = alpha_block(r, first + row)
            return carry

        lax.fori_loop(0, share // group, some, 0)

    def exchange(o, r):
        return pltpu.make_async_remote_copy(
            src_ref=tsend.at[o - 1, r],
            dst_ref=trecv.at[o - 1, r],
            send_sem=tsend_sem.at[o - 1, r],
            recv_sem=trecv_sem.at[o - 1, r],
            device_id={"str": me, "chol": (core + o) % nchol},
            device_id_type=MESH,
        )

    def store(r):
        return pltpu.make_async_copy(out.at[r], out_hbm.at[r], out_sem.at[r])

    def finish(r):
        for o in range(1, nchol):
            exchange(o, r).wait_recv()
            out[r] += trecv[o - 1, r]
        store(r).start()

    for r in range(nvec):
        if n > 1:
            landed = recv[r].at[pl.ds(0, n - 1)]
            pltpu.make_async_copy(landed, landed, recv_sem.at[r]).wait()
        for o in range(1, nchol):
            alpha_rows(tsend.at[o - 1, r], r, ((core + o) % nchol) * share)
            exchange(o, r).start()
        alpha_rows(out.at[r], r, core * share)
        finish(r)

    for r in range(nvec):
        if n > 1:
            sent = send.at[r, pl.ds(0, n - 1)]
            pltpu.make_async_copy(sent, sent, send_sem.at[r]).wait()
        for o in range(1, nchol):
            exchange(o, r).wait_send()
        store(r).wait()


def body(n, nchol, amplitudes, alpha_values, alpha_cols, beta_values, beta_cols):
    nvec, rows, width = amplitudes.shape
    _, nblk, nnz, blk, _ = beta_values.shape
    assert rows == blk and width == n * blk and nblk == n
    out_rows = nblk * blk // nchol
    dma = pltpu.SemaphoreType.DMA
    others = max(nchol - 1, 1)
    half = (n, blk, blk)
    smem = pl.BlockSpec(memory_space=pltpu.SMEM)
    hbm = pl.BlockSpec(memory_space=pltpu.HBM)
    return pl.pallas_call(
        functools.partial(kernel, n, nchol, nvec, nblk, nnz, blk),
        out_shape=jax.ShapeDtypeStruct((nvec, out_rows, blk), jnp.float32),
        in_specs=[smem, smem, hbm, hbm, hbm],
        out_specs=hbm,
        scratch_shapes=[
            pltpu.VMEM((nblk, nvec, blk, blk), jnp.bfloat16),
            pltpu.VMEM(alpha_values.shape[1:], jnp.bfloat16),
            pltpu.VMEM(beta_values.shape[1:], jnp.bfloat16),
            pltpu.VMEM((nvec,) + half, jnp.bfloat16),
            pltpu.VMEM((others, nvec, out_rows, blk), jnp.float32),
            pltpu.VMEM((others, nvec, out_rows, blk), jnp.float32),
            pltpu.VMEM((nvec, out_rows, blk), jnp.float32),
            *[pltpu.VMEM(half, jnp.bfloat16) for _ in range(nvec)],
            dma((nblk,)), dma, dma((n,)), dma((nvec,)), dma((nvec,)),
            dma((others, nvec)), dma((others, nvec)), dma((nvec,)),
        ],
        compiler_params=pltpu.CompilerParams(
            collective_id=0, has_side_effects=True, vmem_limit_bytes=51 * 1024 * 1024
        ),
        cost_estimate=pl.CostEstimate(
            flops=8 * nvec * nblk * nnz * blk**3, bytes_accessed=2**24, transcendentals=0
        ),
    )(alpha_cols[0].T, beta_cols[0].T, amplitudes, alpha_values[0], beta_values[0])


def solution(mesh):
    placed = (
        P(None, "str", None),
        P("chol", None, None, None, None),
        P("chol", None, None),
        P("chol", None, None, None, None),
        P("chol", None, None),
    )
    return jax.shard_map(
        functools.partial(body, mesh.shape["str"], mesh.shape["chol"]),
        mesh=mesh, in_specs=placed, out_specs=P(None, "chol", "str"), check_vma=False,
    )
```

profile of v0, /device:TPU:0, one launch (start us, length us, event | category | flops | bytes accessed | tf_op | source)
XLA Modules:
  0.0 59.6 jit_solution(7353417477355603869)
XLA Ops:
  0.0 0.0 copy-start
  0.0 0.7 %copy-done = s32[1,16,8]{1,2,0:T(8,128)S(1)} copy-done((s32[1,16,8]{1,2,0:T(8,128)S(1)}, s32[1,16,8]{1,2,0:T(8,128)}, u32[]{:S(2)}) %copy-start) | copy-done | bytes 536
  0.7 0.0 copy-start.1
  0.7 0.7 %copy-done.1 = s32[1,16,8]{1,2,0:T(8,128)S(1)} copy-done((s32[1,16,8]{1,2,0:T(8,128)S(1)}, s32[1,16,8]{1,2,0:T(8,128)}, u32[]{:S(2)}) %copy-start.1) | copy-done | bytes 536
  1.4 56.9 %shard_map.55 = f32[4,1024,128]{2,1,0:T(8,128)S(1)} custom-call(s32[8,16]{1,0:T(8,128)S(1)} %bitcast.8, s32[8,16]{1,0:T(8,128)S(1)} %bitcast.9, bf16[4,128,2048]{2,1,0:T(8,128)(2,1)} %amp_hbm.1, bf16[16,8,128,128]{3,2,1,0:T(8,128)(2,1)} %bitcast.10, bf16[16,8,128,128]{3,2,1,0:T(8,128)(2,1)} %bitcast.11), custom_call_target="tpu_custom_call" | custom-call | flops 8589934592 | bytes 16777216 | tf_op jit(solution)/shard_map/pallas_call | solution.py:213
  58.3 1.3 %copy.7 = f32[4,1024,128]{2,1,0:T(8,128)} copy(f32[4,1024,128]{2,1,0:T(8,128)S(1)} %shard_map.55) | data formatting | bytes 4194304
Async XLA Ops:
  0.0 0.7 %copy-start = (s32[1,16,8]{1,2,0:T(8,128)S(1)}, s32[1,16,8]{1,2,0:T(8,128)}, u32[]{:S(2)}) copy-start(s32[1,16,8]{1,2,0:T(8,128)} %param.7) | copy-start | bytes 1540
  0.7 0.7 %copy-start.1 = (s32[1,16,8]{1,2,0:T(8,128)S(1)}, s32[1,16,8]{1,2,0:T(8,128)}, u32[]{:S(2)}) copy-start(s32[1,16,8]{1,2,0:T(8,128)} %param.9) | copy-start | bytes 1540
where the time goes:
time: 59.9 us; the launch traced here: 59.6 us
  Pallas kernels  56.9 us (95%)
  local copies, waits for them, and re-layouts  2.69 us (4%)
    pallas_call x1, Pallas kernels, body(): pl.pallas_call(functools.partial(kernel, n, nchol, nvec, nblk, nnz, blk),...  56.9 us
    unnamed x5, local copies, waits for them, and re-layouts  2.69 us

commit v1 on v0

--- a/solution.py
+++ b/solution.py
@@ -22,13 +22,15 @@
 
 def kernel(
     n, nchol, nvec, nblk, nnz, blk,
-    acols, bcols, amp_hbm, aval_hbm, bval_hbm, out_hbm,
-    amp, aval, bval, send, tsend, trecv, out, *rest,
+    cols_in, amp_hbm, aval_hbm, bval_hbm, out,
+    cols, amp, aval, bval, send, tsend, trecv, *rest,
 ):
     recv = rest[:nvec]
-    amp_sem, aval_sem, bval_sem, send_sem, recv_sem, tsend_sem, trecv_sem, out_sem = rest[nvec:]
+    cols_sem, amp_sem, aval_sem, bval_sem, send_sem, recv_sem, tsend_sem, trecv_sem = rest[nvec:]
     me, core = lax.axis_index("str"), lax.axis_index("chol")
     share = nblk // nchol
+    group = max(g for g in (4, 2, 1) if share % g == 0)
+    pieces = share // group
 
     barrier = pltpu.get_barrier_semaphore()
 
@@ -43,6 +45,9 @@
         pl.semaphore_signal(
             barrier, inc=1, device_id={"str": me, "chol": (core + o) % nchol}, device_id_type=MESH
         )
+    load_cols = pltpu.make_async_copy(cols_in, cols, cols_sem)
+    load_cols.start()
+
     def load_amp(c):
         return pltpu.make_async_copy(
             amp_hbm.at[:, :, pl.ds(pl.multiple_of(c * blk, blk), blk)], amp.at[c], amp_sem.at[c]
@@ -69,6 +74,7 @@
     load_beta(n - 1, me).start()
     load_alpha = pltpu.make_async_copy(aval_hbm, aval, aval_sem)
 
+    load_cols.wait()
     lax.fori_loop(0, nblk, wait_amp, 0)
     def beta_block(step, j):
         load_beta(step, j).wait()
@@ -76,7 +82,7 @@
         for m in range(0, nnz, 2):
             left, right = [], []
             for b in range(m, min(m + 2, nnz)):
-                left.append(amp[bcols[b, j]].reshape(nvec * blk, blk))
+                left.append(amp[cols[nnz + b, j]].reshape(nvec * blk, blk))
                 right.append(bval[j, b])
             part = lax.dot_general(
                 jnp.concatenate(left, axis=1), jnp.concatenate(right, axis=1),
@@ -148,56 +154,55 @@
 
     def alpha_block(r, i):
         left = jnp.concatenate([aval[i, m] for m in range(nnz)], axis=1)
-        right = jnp.concatenate([recv[r][acols[m, i]] for m in range(nnz)], axis=0)
+        right = jnp.concatenate([recv[r][cols[m, i]] for m in range(nnz)], axis=0)
         return jnp.dot(left, right, preferred_element_type=jnp.float32)
 
-    def alpha_rows(to, r, first):
-        group = max(g for g in (4, 2, 1) if share % g == 0)
-
-        def some(at, carry):
-            for b in range(group):
-                row = at * group + b
-                to[pl.ds(pl.multiple_of(row * blk, blk), blk), :] = alpha_block(r, first + row)
-            return carry
-
-        lax.fori_loop(0, share // group, some, 0)
-
-    def exchange(o, r):
+    def alpha_rows(to, r, first, at):
+        for b in range(group):
+            row = at * group + b
+            to[pl.ds(pl.multiple_of(row * blk, blk), blk), :] = alpha_block(r, first + row)
+
+    def exchange(o, r, at):
+        rows = pl.ds(pl.multiple_of(at * group * blk, group * blk), group * blk)
         return pltpu.make_async_remote_copy(
-            src_ref=tsend.at[o - 1, r],
-            dst_ref=trecv.at[o - 1, r],
-            send_sem=tsend_sem.at[o - 1, r],
-            recv_sem=trecv_sem.at[o - 1, r],
+            src_ref=tsend.at[o - 1, r, rows, :],
+            dst_ref=trecv.at[o - 1, r, rows, :],
+            send_sem=tsend_sem.at[o - 1, r, at],
+            recv_sem=trecv_sem.at[o - 1, r, at],
             device_id={"str": me, "chol": (core + o) % nchol},
             device_id_type=MESH,
         )
-
-    def store(r):
-        return pltpu.make_async_copy(out.at[r], out_hbm.at[r], out_sem.at[r])
-
-    def finish(r):
-        for o in range(1, nchol):
-            exchange(o, r).wait_recv()
-            out[r] += trecv[o - 1, r]
-        store(r).start()
 
     for r in range(nvec):
         if n > 1:
             landed = recv[r].at[pl.ds(0, n - 1)]
             pltpu.make_async_copy(landed, landed, recv_sem.at[r]).wait()
         for o in range(1, nchol):
-            alpha_rows(tsend.at[o - 1, r], r, ((core + o) % nchol) * share)
-            exchange(o, r).start()
-        alpha_rows(out.at[r], r, core * share)
-        finish(r)
+            def theirs(at, carry, o=o, r=r):
+                alpha_rows(tsend.at[o - 1, r], r, ((core + o) % nchol) * share, at)
+                exchange(o, r, at).start()
+                return carry
+
+            lax.fori_loop(0, pieces, theirs, 0)
+
+        def ours(at, carry, r=r):
+            alpha_rows(out.at[r], r, core * share, at)
+            return carry
+
+        lax.fori_loop(0, pieces, ours, 0)
+        for o in range(1, nchol):
+            for at in range(pieces):
+                exchange(o, r, at).wait_recv()
+                rows = pl.ds(at * group * blk, group * blk)
+                out[r, rows, :] += trecv[o - 1, r, rows, :]
 
     for r in range(nvec):
         if n > 1:
             sent = send.at[r, pl.ds(0, n - 1)]
             pltpu.make_async_copy(sent, sent, send_sem.at[r]).wait()
         for o in range(1, nchol):
-            exchange(o, r).wait_send()
-        store(r).wait()
+            for at in range(pieces):
+                exchange(o, r, at).wait_send()
 
 
 def body(n, nchol, amplitudes, alpha_values, alpha_cols, beta_values, beta_cols):
@@ -205,27 +210,29 @@
     _, nblk, nnz, blk, _ = beta_values.shape
     assert rows == blk and width == n * blk and nblk == n
     out_rows = nblk * blk // nchol
+    cols = jnp.concatenate([alpha_cols[0].T, beta_cols[0].T], axis=0)
     dma = pltpu.SemaphoreType.DMA
     others = max(nchol - 1, 1)
+    share = nblk // nchol
+    pieces = share // max(g for g in (4, 2, 1) if share % g == 0)
     half = (n, blk, blk)
-    smem = pl.BlockSpec(memory_space=pltpu.SMEM)
     hbm = pl.BlockSpec(memory_space=pltpu.HBM)
     return pl.pallas_call(
         functools.partial(kernel, n, nchol, nvec, nblk, nnz, blk),
         out_shape=jax.ShapeDtypeStruct((nvec, out_rows, blk), jnp.float32),
-        in_specs=[smem, smem, hbm, hbm, hbm],
-        out_specs=hbm,
+        in_specs=[hbm, hbm, hbm, hbm],
+        out_specs=pl.BlockSpec(memory_space=pltpu.VMEM),
         scratch_shapes=[
+            pltpu.SMEM(cols.shape, jnp.int32),
             pltpu.VMEM((nblk, nvec, blk, blk), jnp.bfloat16),
             pltpu.VMEM(alpha_values.shape[1:], jnp.bfloat16),
             pltpu.VMEM(beta_values.shape[1:], jnp.bfloat16),
             pltpu.VMEM((nvec,) + half, jnp.bfloat16),
             pltpu.VMEM((others, nvec, out_rows, blk), jnp.float32),
             pltpu.VMEM((others, nvec, out_rows, blk), jnp.float32),
-            pltpu.VMEM((nvec, out_rows, blk), jnp.float32),
             *[pltpu.VMEM(half, jnp.bfloat16) for _ in range(nvec)],
-            dma((nblk,)), dma, dma((n,)), dma((nvec,)), dma((nvec,)),
-            dma((others, nvec)), dma((others, nvec)), dma((nvec,)),
+            dma, dma((nblk,)), dma, dma((n,)), dma((nvec,)), dma((nvec,)),
+            dma((others, nvec, pieces)), dma((others, nvec, pieces)),
         ],
         compiler_params=pltpu.CompilerParams(
             collective_id=0, has_side_effects=True, vmem_limit_bytes=51 * 1024 * 1024
@@ -233,7 +240,7 @@
         cost_estimate=pl.CostEstimate(
             flops=8 * nvec * nblk * nnz * blk**3, bytes_accessed=2**24, transcendentals=0
         ),
-    )(alpha_cols[0].T, beta_cols[0].T, amplitudes, alpha_values[0], beta_values[0])
+    )(cols, amplitudes, alpha_values[0], beta_values[0])
 
 
 def solution(mesh):

time: 59.9 us -> 58.1 us (0.970)
  local copies, waits for them, and re-layouts: 2.69 us -> 1.32 us
  Pallas kernels: 56.9 us -> 55.8 us
  other arithmetic: 0 us -> 0.71 us
    unnamed x5 -> x1, local copies, waits for them, and re-layouts: 2.69 us -> 1.32 us
    pallas_call x1, Pallas kernels: 56.9 us -> 55.8 us  [body(): pl.pallas_call(functools.partial(kernel, n, nchol, nvec, nblk, nnz, blk),...]
    concatenate x0 -> x1, other arithmetic: none -> 0.71 us  [body(): cols = jnp.concatenate([alpha_cols[0].T, beta_cols[0].T], axis=0)]
where the time goes in v1:
time: 58.1 us; the launch traced here: 57.9 us
  Pallas kernels  55.8 us (96%)
  local copies, waits for them, and re-layouts  1.32 us (2%)
  other arithmetic  0.71 us (1%)
    pallas_call x1, Pallas kernels, body(): pl.pallas_call(functools.partial(kernel, n, nchol, nvec, nblk, nnz, blk),...  55.8 us
    unnamed x1, local copies, waits for them, and re-layouts  1.32 us

profile of v1, /device:TPU:0, one launch (start us, length us, event | category | flops | bytes accessed | tf_op | source)
XLA Modules:
  0.0 57.9 jit_solution(7606786808205407034)
XLA Ops:
  0.0 0.7 %pad_add_fusion.cols_in = s32[16,16]{1,0:T(8,128)S(1)} fusion(s32[8,16]{1,0:T(8,128)} %bitcast.8, s32[8,16]{1,0:T(8,128)} %bitcast.9), kind=kLoop, calls=%fused_computation | loop fusion | flops 256 | bytes 2048 | tf_op jit(solution)/shard_map/concatenate | solution.py:213
  0.7 55.8 %shard_map.55 = f32[4,1024,128]{2,1,0:T(8,128)S(1)} custom-call(s32[16,16]{1,0:T(8,128)S(1)} %pad_add_fusion.cols_in, bf16[4,128,2048]{2,1,0:T(8,128)(2,1)} %amp_hbm.1, bf16[16,8,128,128]{3,2,1,0:T(8,128)(2,1)} %bitcast.10, bf16[16,8,128,128]{3,2,1,0:T(8,128)(2,1)} %bitcast.11), custom_call_target="tpu_custom_call" | custom-call | flops 8589934592 | bytes 16777216 | tf_op jit(solution)/shard_map/pallas_call | solution.py:220
  56.5 1.3 %copy.7 = f32[4,1024,128]{2,1,0:T(8,128)} copy(f32[4,1024,128]{2,1,0:T(8,128)S(1)} %shard_map.55) | data formatting | bytes 4194304
